TPU v7x, 32 devices: a whole 2x2x4 slice. The times are simulated.
32 devices in a mesh: fsdp: 16 (over z, y, core), tp: 2 (over x).
Axes of the slice: x: 2, y: 2, z: 4, core: 2. Of those that a mesh axis runs over, the one named last changes fastest.
Arguments:
- tokens: bfloat16 [4096, 4096], P('fsdp', 'tp'), may hold values from -6 to 6
- w_feat: bfloat16 [3, 4096, 4096], P(None, 'fsdp', 'tp'), may hold values from -0.09375 to 0.09375
- short_filter: float32 [3, 256, 7], P(None, 'tp'), may hold values from -6 to 6
- long_filter: bfloat16 [256, 128], P('tp'), may hold values from -1.5 to 1.5
- doc_ids: int32 [4096], P('fsdp'), may hold values from 0 to 7, never falling along the last dimension, each value on 1 to 2048 neighbouring positions
- grad_out: bfloat16 [4096, 4096], P('fsdp', 'tp'), may hold values from -6 to 6
Outputs:
- mixed: bfloat16 [4096, 4096], P('fsdp', 'tp')
- input_grad: bfloat16 [4096, 4096], P('fsdp', 'tp')
Inputs may be any that keep to these rules, and one draw needn't show every extreme that they name: `doc_ids`: document numbers never fall along the positions; each document covers 1 to 2048 consecutive positions and one covers exactly 2048; every number from 0 to 7 occurs.
All inputs are finite; a program needn't handle non-finite values.
Results may differ from a plain program's by a relative error of at most 0.0081.
Values may be sent and summed in bfloat16 or wider, within the bound.
A program may use at most 192 MiB of HBM per device.

v0:
```python
import jax
import jax.numpy as jnp
from jax import lax
from jax.sharding import PartitionSpec as P


def shifted_2(value, axis, steps):
    count = lax.axis_size(axis)
    initial, last = (max(0, -steps), min(count, count - steps))
    return lax.ppermute(value, axis, [(source, source + steps) for source in range(initial, last)])


def causal_taps(extended, doc_ext, filters, lead_rows):
    row_count = extended.shape[0] - lead_rows
    doc_now = doc_ext[lead_rows:]
    bcast_shape = (row_count,) + (1,) * (extended.ndim - 1)
    summed = jnp.zeros((row_count,) + extended.shape[1:], jnp.float32)
    for offset in range(filters.shape[-1]):
        shifted = extended[lead_rows - offset : lead_rows - offset + row_count].astype(jnp.float32)
        same_doc = (
            (doc_ext[lead_rows - offset : lead_rows - offset + row_count] == doc_now)
            .astype(jnp.float32)
            .reshape(bcast_shape)
        )
        summed = summed + filters[..., offset] * shifted * same_doc
    return summed


def ahead_taps(extended, doc_ext, filters, row_count):
    doc_now = doc_ext[:row_count]
    bcast_shape = (row_count,) + (1,) * (extended.ndim - 1)
    summed = jnp.zeros((row_count,) + extended.shape[1:], jnp.float32)
    for offset in range(filters.shape[-1]):
        shifted = extended[offset : offset + row_count].astype(jnp.float32)
        same_doc = (
            (doc_ext[offset : offset + row_count] == doc_now)
            .astype(jnp.float32)
            .reshape(bcast_shape)
        )
        summed = summed + filters[..., offset] * shifted * same_doc
    return summed


def toeplitz_base(long_filter, anti_causal):
    tap_count = long_filter.shape[1]
    row_iota = lax.broadcasted_iota(jnp.int32, (tap_count, 2 * tap_count), 0)
    col_iota = lax.broadcasted_iota(jnp.int32, (tap_count, 2 * tap_count), 1)
    if anti_causal:
        lag_index = col_iota - row_iota
    else:
        lag_index = row_iota + tap_count - col_iota
    tap_iota = lax.broadcasted_iota(jnp.int32, (tap_count, tap_count, 2 * tap_count), 0)
    one_hot = (
        (tap_iota == lag_index[None])
        .astype(long_filter.dtype)
        .reshape(tap_count, 2 * tap_count * tap_count)
    )
    table = jnp.dot(long_filter, one_hot, preferred_element_type=jnp.float32).astype(
        long_filter.dtype
    )
    return table.reshape(long_filter.shape[0], tap_count, 2 * tap_count)


def blocked_conv(extended, doc_ext, toeplitz, doc_rows, row_count):
    groups = toeplitz.shape[0]
    tap_count = toeplitz.shape[1]
    chan_width = extended.shape[1]
    block_count = row_count // tap_count
    row_blocks = extended.reshape(block_count + 1, tap_count, chan_width)
    windows = jnp.concatenate([row_blocks[:-1], row_blocks[1:]], axis=1)
    doc_blocks = doc_ext.reshape(block_count + 1, tap_count)
    doc_windows = jnp.concatenate([doc_blocks[:-1], doc_blocks[1:]], axis=1)
    row_docs = doc_rows.reshape(block_count, tap_count)

    def one_block(inputs):
        window, col_docs, own_docs = inputs
        window = window.reshape(2 * tap_count, groups, chan_width // groups)
        kernel = toeplitz * (own_docs[:, None] == col_docs[None, :]).astype(toeplitz.dtype)[None]
        result = jnp.einsum("gtu,ugk->tgk", kernel, window, preferred_element_type=jnp.float32)
        return result.reshape(tap_count, chan_width)

    blocks = lax.map(one_block, (windows, doc_windows, row_docs))
    return blocks.reshape(row_count, chan_width)


def shards(tokens, w_feat, short_filter, long_filter, doc_ids, grad_out):
    rows_here = tokens.shape[0]
    tap_count = long_filter.shape[1]
    margin = 8
    reach_rows = tap_count + margin
    gathered = lax.all_gather(tokens, "tp", axis=1, tiled=True)
    filter_groups = short_filter.shape[1]
    short_full = jnp.broadcast_to(
        short_filter[:, :, None, :], (3, filter_groups, 16, short_filter.shape[2])
    ).reshape(3, filter_groups * 16, short_filter.shape[2])
    w_whole = lax.all_gather(w_feat, "fsdp", axis=1, tiled=True)
    u_all = jnp.einsum("sd,jdc->sjc", gathered, w_whole, preferred_element_type=jnp.float32).astype(
        jnp.bfloat16
    )
    u_pair = u_all[:, 1:]
    prev_pair, prev_doc = shifted_2(
        (u_pair[rows_here - reach_rows :], doc_ids[rows_here - reach_rows :]), "fsdp", 1
    )
    ext_pair = jnp.concatenate([prev_pair, u_pair], axis=0)
    ext_doc = jnp.concatenate([prev_doc, doc_ids], axis=0)
    conv_pair = causal_taps(ext_pair, ext_doc, short_full[1:], margin)
    product_kv = (conv_pair[:, 0] * conv_pair[:, 1]).astype(jnp.bfloat16)
    doc_product = ext_doc[margin:]
    long_out = blocked_conv(
        product_kv, doc_product, toeplitz_base(long_filter, False), doc_ids, rows_here
    )
    conv_pair, long_out, prev_doc = (
        conv_pair[tap_count:],
        long_out,
        prev_doc[reach_rows - margin :],
    )
    u_query = u_all[:, 0]
    prev_query = shifted_2(u_query[rows_here - margin :], "fsdp", 1)
    ext_query = jnp.concatenate([prev_query, u_query], axis=0)
    ext_doc = jnp.concatenate([prev_doc, doc_ids], axis=0)
    conv_query = causal_taps(ext_query, ext_doc, short_full[0], margin)
    pieces = ((0, 3, w_whole),)
    block_out = (conv_query * long_out).astype(jnp.bfloat16)
    grad_float = grad_out.astype(jnp.float32)
    grad_long = (grad_float * conv_query).astype(jnp.bfloat16)
    grad_query = grad_float * long_out
    next_grad, next_doc = shifted_2((grad_long[:tap_count], doc_ids[:tap_count]), "fsdp", -1)
    ext_grad = jnp.concatenate([grad_long, next_grad], axis=0)
    ext_doc = jnp.concatenate([doc_ids, next_doc], axis=0)
    grad_mixed = blocked_conv(
        ext_grad, ext_doc, toeplitz_base(long_filter, True), doc_ids, rows_here
    )
    grad_feat = jnp.stack(
        [grad_query, grad_mixed * conv_pair[:, 1], grad_mixed * conv_pair[:, 0]], axis=1
    ).astype(jnp.bfloat16)
    next_feat = shifted_2(grad_feat[:margin], "fsdp", -1)
    ext_feat = jnp.concatenate([grad_feat, next_feat], axis=0)
    doc_feat = jnp.concatenate([doc_ids, next_doc[:margin]], axis=0)
    grad_u = ahead_taps(ext_feat, doc_feat, short_full, rows_here).astype(jnp.bfloat16)
    first_role, end_role, weights = pieces[0]
    partial_value = jnp.einsum("sjc,jdc->sd", grad_u, weights, preferred_element_type=jnp.float32)
    input_grad = lax.psum_scatter(
        partial_value.astype(jnp.bfloat16), "tp", scatter_dimension=1, tiled=True
    )
    return (block_out, input_grad)


def solution(mesh):
    in_specs = (
        P("fsdp", "tp"),
        P(None, "fsdp", "tp"),
        P(None, "tp", None),
        P("tp", None),
        P("fsdp"),
        P("fsdp", "tp"),
    )
    out_specs = (P("fsdp", "tp"), P("fsdp", "tp"))
    return jax.shard_map(shards, mesh=mesh, in_specs=in_specs, out_specs=out_specs, check_vma=False)
```

profile of v0, /device:TPU:0, one launch (start us, length us, event | category | flops | bytes accessed | tf_op | source)
XLA Modules:
  0.0 490.7 jit_solution(5397390255139693855)
XLA Ops:
  8.0 0.7 all-gather.5.cloned.1.call-update
  8.8 2.3 collective-permute-start.1
  11.2 1.3 collective-permute-start.4
  14.4 0.8 reshape.228
  15.6 4.7 convolution_convert_fusion
  20.4 4.6 convolution_convert_fusion.1
  25.0 12.7 %copy.35 = bf16[128,128,256]{2,1,0:T(8,128)(2,1)} copy(bf16[128,128,256]{0,2,1:T(8,128)(2,1)} %bitcast.135) | data formatting | bytes 16777216 | tf_op jit(solution)/shard_map/while | solution.py:82
  37.7 12.7 %copy.31 = bf16[128,128,256]{2,1,0:T(8,128)(2,1)} copy(bf16[128,128,256]{0,2,1:T(8,128)(2,1)} %bitcast.136) | data formatting | bytes 16777216 | tf_op jit(solution)/shard_map/while | solution.py:82
  50.7 243.4 %all-gather.5.cloned.1.call-done = bf16[3,4096,2048]{2,1,0:T(8,128)(2,1)} async-done(((bf16[3,256,2048]{2,1,0:T(8,128)(2,1)}), bf16[3,4096,2048]{2,1,0:T(8,128)(2,1)}) %all-gather.5.cloned.1.call-update) | async-done | bytes 50331664 | tf_op jit(solution)/shard_map/all_gather | solution.py:96
  294.1 21.2 %convolution_convert_fusion.2 = bf16[256,3,2048]{2,0,1:T(8,128)(2,1)S(1)} fusion(bf16[3,4096,2048]{2,1,0:T(8,128)(2,1)} %all-gather.5.cloned.1.call-done, bf16[256,4096]{1,0:T(8,128)(2,1)} %all-gather.3.cloned.1.call-done), kind=kOutput, calls=%fused_computation.42 | convolution fusion | flops 12886474752 | bytes 55574528 | tf_op jit(solution)/shard_map/sd,jdc->sjc/dot_general | solution.py:97
  315.4 2.2 collective-permute-start
  317.6 0.7 collective-permute-done
  318.4 4.0 fusion.42
  322.4 1.5 collective-permute-start.3
  324.0 1.1 slice.412
  325.1 1.5 slice.413
  326.6 4.5 collective-permute-start.2
  331.7 1.1 pad_maximum_fusion.5
  333.5 1.6 pad_maximum_fusion.4
  335.1 1.6 broadcast.89.clone2.1
  336.7 17.0 %while.21 = (s32[]{:T(128)}, f32[2,128,2048]{2,1,0:T(8,128)}, bf16[2,256,2048]{1,2,0:T(8,128)(2,1)}, s32[2,128]{1,0:T(2,128)S(1)}, s32[2,256]{1,0:T(2,128)S(1)}, /*index=5*/bf16[128,128,256]{2,1,0:T(8,128)(2,1)}, s32[]{:T(128)}) while((s32[]{:T(128)}, f32[2,128,2048]{2,1,0:T(8,128)}, bf16[2,256,2048]{1,2,0:T(8,128)(2,1)}, ...), condition=%wide.region_3.4_spmd, body=%wide.region_2.3_spmd.sunk | while | flops 138477568 | bytes 16913496 | solution.py:82
  336.8 1.3 constant_dynamic-slice_fusion.12
  338.1 5.7 %fusion.83 = f32[128,16,128]{2,1,0:T(8,128)S(1)} fusion(bf16[256,128,16]{0,2,1:T(8,128)(2,1)S(1)} %bitcast.131, bf16[128,128,256]{2,1,0:T(8,128)(2,1)} %get-tuple-element.307, bf16[128,256]{1,0:T(8,128)(2,1)S(1)} %compare_convert_fusion.17), kind=kOutput, calls=%fused_computation.9.clone.1 | convolution fusion | flops 138412032 | bytes 10551296 | tf_op jit(solution)/shard_map/while/body/eval_jaxpr/gtu,ugk->tgk/dot_general | solution.py:79
  344.2 1.1 constant_dynamic-update-slice_fusion.5
  345.3 1.3 constant_dynamic-slice_fusion.12
  346.6 5.7 %fusion.83 = f32[128,16,128]{2,1,0:T(8,128)S(1)} fusion(bf16[256,128,16]{0,2,1:T(8,128)(2,1)S(1)} %bitcast.131, bf16[128,128,256]{2,1,0:T(8,128)(2,1)} %get-tuple-element.307, bf16[128,256]{1,0:T(8,128)(2,1)S(1)} %compare_convert_fusion.17), kind=kOutput, calls=%fused_computation.9.clone.1 | convolution fusion | flops 138412032 | bytes 10551296 | tf_op jit(solution)/shard_map/while/body/eval_jaxpr/gtu,ugk->tgk/dot_general | solution.py:79
  352.7 1.1 constant_dynamic-update-slice_fusion.5
  353.8 20.9 %multiply_add_fusion = f32[384,2,2048]{2,0,1:T(8,128)S(1)} fusion(bf16[256,2,2048]{2,0,1:T(8,128)(2,1)} %slice.413, bf16[136,2,2048]{2,0,1:T(8,128)(2,1)} %collective-permute-done.2, f32[384]{0:T(512)S(1)} %get-tuple-element.172, f32[2,2048]{1,0:T(2,128)S(1)} %get-tuple-element.146, f32[384]{0:T(512)S(1)} %get-tuple-element.173, ...), kind=kLoop, calls=%fused_computation.33 | loop fusion | flops 73924608 | bytes 9626624 | tf_op jit(solution)/shard_map/add | solution.py:25
  375.1 1.2 copy-done.3
  376.3 1.7 fusion.44
  378.0 1.2 fusion.58
  379.2 1.6 copy.29
  380.8 1.3 copy.30
  382.1 2.8 pad_maximum_fusion.3
  385.0 1.6 broadcast.89.clone2
  386.5 17.0 %while.20 = (s32[]{:T(128)}, f32[2,128,2048]{2,1,0:T(8,128)}, bf16[2,256,2048]{1,2,0:T(8,128)(2,1)}, s32[2,128]{1,0:T(2,128)S(1)}, s32[2,256]{1,0:T(2,128)S(1)}, /*index=5*/bf16[128,128,256]{2,1,0:T(8,128)(2,1)}, s32[]{:T(128)}) while((s32[]{:T(128)}, f32[2,128,2048]{2,1,0:T(8,128)}, bf16[2,256,2048]{1,2,0:T(8,128)(2,1)}, ...), condition=%wide.region_1.2_spmd, body=%wide.region_0.1_spmd.sunk | while | flops 138477568 | bytes 16913496 | solution.py:82
  386.6 1.3 constant_dynamic-slice_fusion.10
  388.0 5.7 %fusion.79 = f32[128,16,128]{2,1,0:T(8,128)S(1)} fusion(bf16[256,128,16]{0,2,1:T(8,128)(2,1)S(1)} %bitcast.132, bf16[128,128,256]{2,1,0:T(8,128)(2,1)} %get-tuple-element.286, bf16[128,256]{1,0:T(8,128)(2,1)S(1)} %compare_convert_fusion.16), kind=kOutput, calls=%fused_computation.clone.1 | convolution fusion | flops 138412032 | bytes 10551296 | tf_op jit(solution)/shard_map/while/body/eval_jaxpr/gtu,ugk->tgk/dot_general | solution.py:79
  394.0 1.0 constant_dynamic-update-slice_fusion.4
  395.1 1.3 constant_dynamic-slice_fusion.10
  396.4 5.7 %fusion.79 = f32[128,16,128]{2,1,0:T(8,128)S(1)} fusion(bf16[256,128,16]{0,2,1:T(8,128)(2,1)S(1)} %bitcast.132, bf16[128,128,256]{2,1,0:T(8,128)(2,1)} %get-tuple-element.286, bf16[128,256]{1,0:T(8,128)(2,1)S(1)} %compare_convert_fusion.16), kind=kOutput, calls=%fused_computation.clone.1 | convolution fusion | flops 138412032 | bytes 10551296 | tf_op jit(solution)/shard_map/while/body/eval_jaxpr/gtu,ugk->tgk/dot_general | solution.py:79
  402.4 1.1 constant_dynamic-update-slice_fusion.4
  403.5 4.2 fusion.41
  408.0 1.3 collective-permute-start.5
  409.4 4.1 collective-permute-done.5
  413.5 1.9 pad_maximum_fusion
  415.4 31.4 %fusion.14 = bf16[256,4096]{1,0:T(8,128)(2,1)} fusion(bf16[3,4096,2048]{2,1,0:T(8,128)(2,1)} %all-gather.5.cloned.1.call-done, bf16[264,3,2048]{2,0,1:T(8,128)(2,1)} %pad_maximum_fusion, f32[256]{0:T(256)S(1)} %get-tuple-element.163, f32[3,2048]{1,0:T(4,128)S(1)} %get-tuple-element.187, f32[256]{0:T(256)S(1)} %get-tuple-element.164, ...), kind=kOutput, calls=%fused_computation.35 | convolution fusion | flops 12931563520 | bytes 74627072 | tf_op jit(solution)/shard_map/sjc,jdc->sd/dot_general | solution.py:141
  446.8 37.3 %reduce-scatter.2.cloned.1.call-done = bf16[256,2048]{1,0:T(8,128)(2,1)} async-done(((bf16[256,4096]{1,0:T(8,128)(2,1)}), bf16[256,2048]{1,0:T(8,128)(2,1)}) %reduce-scatter.2.cloned.1.call-update) | async-done | bytes 1048592 | tf_op jit(solution)/shard_map/reduce_scatter | solution.py:142
  (81 shorter events, 7.7 us)
Async XLA Ops:
  7.2 8.5 %copy-start = (bf16[128,128]{1,0:T(8,128)(2,1)S(1)}, bf16[128,128]{1,0:T(8,128)(2,1)}, u32[]{:S(2)}) copy-start(bf16[128,128]{1,0:T(8,128)(2,1)} %param.13) | copy-start | bytes 98308
  7.2 1.6 copy-start.6
  7.2 5.3 %copy-start.5 = (f32[3,128,7]{1,2,0:T(8,128)S(1)}, f32[3,128,7]{1,2,0:T(8,128)}, u32[]{:S(2)}) copy-start(f32[3,128,7]{1,2,0:T(8,128)} %param.12) | copy-start | bytes 32260
  7.2 5.9 %slice-start = ((f32[3,128,7]{1,2,0:T(8,128)}), f32[2,128,7]{1,2,0:T(8,128)S(1)}, s32[]{:S(2)}) async-start(f32[3,128,7]{1,2,0:T(8,128)} %param.12), calls=%async_computation.4 | async-start | bytes 16384 | tf_op jit(solution)/shard_map/slice | solution.py:106
  7.2 43.5 %all-gather.3.cloned.1.call-start = ((), (), s32[]{:S(2)}) async-start(), calls=%async_computation.1 | async-start | bytes 3145728 | tf_op jit(solution)/shard_map/all_gather | solution.py:91
  7.9 286.2 %all-gather.5.cloned.1.call-start = ((), (), s32[]{:S(2)}) async-start(), calls=%async_computation.2 | async-start | bytes 53477376 | tf_op jit(solution)/shard_map/all_gather | solution.py:96
  8.7 475.5 %reduce-scatter.2.cloned.1.call-start = ((), (), s32[]{:S(2)}) async-start(), calls=%async_computation.3 | async-start | bytes 3145728 | tf_op jit(solution)/shard_map/reduce_scatter | solution.py:142
  8.8 41.5 %collective-permute-start.1 = (s32[136]{0:T(256)S(1)}, s32[136]{0:T(256)S(1)}, u32[]{:S(2)}, u32[]{:S(2)}) collective-permute-start(s32[136]{0:T(256)S(1)} %slice.310), channel_id=1, source_target_pairs={{0,2},{2,4},{4,6},{6,8},{8,10},{10,12},{12,14},{14,16},{16,18},{18... | collective-permute-start | bytes 1640 | tf_op jit(solution)/shard_map/ppermute | solution.py:10
  11.2 39.2 %collective-permute-start.4 = (s32[128]{0:T(128)S(1)}, s32[128]{0:T(128)S(1)}, u32[]{:S(2)}, u32[]{:S(2)}) collective-permute-start(s32[128]{0:T(128)S(1)} %slice.367), channel_id=1, source_target_pairs={{2,0},{4,2},{6,4},{8,6},{10,8},{12,10},{14,12},{16,14},{18,16},{20... | collective-permute-start | bytes 1544 | tf_op jit(solution)/shard_map/ppermute | solution.py:10
  50.6 267.7 %copy-start.4 = (bf16[256,2048]{1,0:T(8,128)(2,1)S(1)}, bf16[256,2048]{1,0:T(8,128)(2,1)}, u32[]{:S(2)}) copy-start(bf16[256,2048]{1,0:T(8,128)(2,1)} %param.15) | copy-start | bytes 3145732
  315.4 3.0 collective-permute-start
  322.4 9.4 %collective-permute-start.3 = (bf16[128,2048]{1,0:T(8,128)(2,1)S(1)}, bf16[128,2048]{1,0:T(8,128)(2,1)}, u32[]{:S(2)}, u32[]{:S(2)}) collective-permute-start(bf16[128,2048]{1,0:T(8,128)(2,1)S(1)} %slice.437), channel_id=1, source_target_pairs={{2,0},{4,2},{6,4},{8,6},{10,8},{12,10},{14,12},{16,14},{18,16},{20... | collective-permute-start | bytes 1572872 | tf_op jit(solution)/shard_map/ppermute | solution.py:10
  326.6 27.2 %collective-permute-start.2 = (bf16[136,2,2048]{2,0,1:T(8,128)(2,1)}, bf16[136,2,2048]{2,0,1:T(8,128)(2,1)}, u32[]{:S(2)}, u32[]{:S(2)}) collective-permute-start(bf16[136,2,2048]{2,0,1:T(8,128)(2,1)} %slice.412), channel_id=1, source_target_pairs={{0,2},{2,4},{4,6},{6,8},{8,10},{10,12},{12,14},{14,16},{16,18},{18... | collective-permute-start | bytes 3342344 | tf_op jit(solution)/shard_map/ppermute | solution.py:10
  374.7 1.6 copy-start.3
  403.5 4.2 copy-start.2
  408.0 5.5 %collective-permute-start.5 = (bf16[8,3,2048]{2,0,1:T(8,128)(2,1)S(1)}, bf16[8,3,2048]{2,0,1:T(8,128)(2,1)S(1)}, u32[]{:S(2)}, u32[]{:S(2)}) collective-permute-start(bf16[8,3,2048]{2,0,1:T(8,128)(2,1)S(1)} %slice.441), channel_id=1, source_target_pairs={{2,0},{4,2},{6,4},{8,6},{10,8},{12,10},{14,12},{16,14},{18,16},{20... | collective-permute-start | bytes 294920 | tf_op jit(solution)/shard_map/ppermute | solution.py:10
  415.4 68.7 %copy-start.1 = (bf16[128,128]{1,0:T(8,128)(2,1)S(1)}, bf16[128,128]{1,0:T(8,128)(2,1)}, u32[]{:S(2)}) copy-start(bf16[128,128]{1,0:T(8,128)(2,1)} %param.13) | copy-start | bytes 98308
Sparse Core Ops, SparseCore 0:
  9.6 35.8 all-gather.2
  47.0 247.0 all-gather.4
  446.9 37.1 reduce-scatter.1
where the time goes:
time: 492 us; the launch traced here: 491 us
  waiting for transfers between devices  287 us (58%)
  matrix products  84.6 us (17%)
  local copies, waits for them, and re-layouts  52.1 us (11%)
  other arithmetic  39.6 us (8%)
  between operations  14.1 us (3%)
  starting transfers between devices  13.2 us (3%)
    all_gather x1, waiting for transfers between devices, shards(): w_whole = lax.all_gather(w_feat, 'fsdp', axis=1, tiled=True)  243 us
    reduce_scatter x1, waiting for transfers between devices, shards(): lax.psum_scatter(partial_value.astype(jnp.bfloat16), 'tp', scatter_dimens...  37.3 us
    dot_general x1, matrix products, shards(): jnp.einsum('sjc,jdc->sd', grad_u, weights, preferred_element_type=jnp.flo...  31.4 us
    while x2, local copies, waits for them, and re-layouts, blocked_conv(): blocks = lax.map(one_block, (windows, doc_windows, row_docs))  25.4 us
    dot_general x4, matrix products, one_block(): jnp.einsum('gtu,ugk->tgk', kernel, window, preferred_element_type=jnp.flo...  22.6 us
    dot_general x1, matrix products, shards(): jnp.einsum('sd,jdc->sjc', gathered, w_whole, preferred_element_type=jnp.f...  21.2 us
    add x1, other arithmetic, causal_taps(): summed = summed + filters[..., offset] * shifted * same_doc  20.9 us
    ppermute x6, starting transfers between devices, shifted_2(): lax.ppermute(value, axis, [(source, source + steps) for source in range(i...  13.1 us
  transfers between devices with their start and end apart: 9, of which 4 were waited for; matrix products, arithmetic and copies ran while one was open for 13% of the time, Pallas kernels for 0%

commit v1 on v0

--- a/solution.py
+++ b/solution.py
@@ -93,7 +93,12 @@
     short_full = jnp.broadcast_to(
         short_filter[:, :, None, :], (3, filter_groups, 16, short_filter.shape[2])
     ).reshape(3, filter_groups * 16, short_filter.shape[2])
-    w_whole = lax.all_gather(w_feat, "fsdp", axis=1, tiled=True)
+    ring = [w_feat]
+    for hop in range(15):
+        ring.append(lax.ppermute(ring[-1], "fsdp", [(dev, (dev + 1) % 16) for dev in range(16)]))
+    w_whole = jnp.roll(
+        jnp.concatenate(ring[::-1], axis=1), (lax.axis_index("fsdp") + 1) * ring[0].shape[1], axis=1
+    )
     u_all = jnp.einsum("sd,jdc->sjc", gathered, w_whole, preferred_element_type=jnp.float32).astype(
         jnp.bfloat16
     )

time: 492 us -> 915 us (1.86)
  waiting for transfers between devices: 287 us -> 573 us
  local copies, waits for them, and re-layouts: 52.1 us -> 168 us
  matrix products: 84.6 us -> 97 us
    ppermute x0 -> x15, waiting for transfers between devices: none -> 529 us  [shards(): lax.ppermute(ring[-1], 'fsdp', [(dev, (dev + 1) % 16) for dev in range(16)])]
    all_gather x1 -> x0, waiting for transfers between devices: 243 us -> none  [shards(): w_whole = lax.all_gather(w_feat, 'fsdp', axis=1, tiled=True)]
    unnamed x22 -> x147, local copies, waits for them, and re-layouts: 1.45 us -> 99.1 us
    dot_general x1, matrix products: 21.2 us -> 33.5 us  [shards(): jnp.einsum('sd,jdc->sjc', gathered, w_whole, preferred_element_type=jnp.f...]
  transfers between devices with their start and end apart: 9 -> 23, of which waited for: 4 -> 18; matrix products, arithmetic and copies ran while one was open for 13% -> 18% of each run, Pallas kernels for 0% -> 0%
where the time goes in v1:
time: 915 us; the launch traced here: 910 us
  waiting for transfers between devices  573 us (63%)
  local copies, waits for them, and re-layouts  168 us (18%)
  matrix products  97 us (11%)
  other arithmetic  44.5 us (5%)
  between operations  14.8 us (2%)
  starting transfers between devices  12 us (1%)
    ppermute x15, waiting for transfers between devices, shards(): lax.ppermute(ring[-1], 'fsdp', [(dev, (dev + 1) % 16) for dev in range(16)])  529 us
    unnamed x147, local copies, waits for them, and re-layouts  99.1 us
    reduce_scatter x1, waiting for transfers between devices, shards(): lax.psum_scatter(partial_value.astype(jnp.bfloat16), 'tp', scatter_dimens...  39.5 us
    dot_general x1, matrix products, shards(): jnp.einsum('sd,jdc->sjc', gathered, w_whole, preferred_element_type=jnp.f...  33.5 us
    dot_general x1, matrix products, shards(): jnp.einsum('sjc,jdc->sd', grad_u, weights, preferred_element_type=jnp.flo...  31.5 us
    while x2, local copies, waits for them, and re-layouts, blocked_conv(): blocks = lax.map(one_block, (windows, doc_windows, row_docs))  24.7 us
    dot_general x4, matrix products, one_block(): jnp.einsum('gtu,ugk->tgk', kernel, window, preferred_element_type=jnp.flo...  22.6 us
    add x1, other arithmetic, causal_taps(): summed = summed + filters[..., offset] * shifted * same_doc  21.3 us
  transfers between devices with their start and end apart: 23, of which 18 were waited for; matrix products, arithmetic and copies ran while one was open for 18% of the time, Pallas kernels for 0%

profile of v1, /device:TPU:0, one launch (start us, length us, event | category | flops | bytes accessed | tf_op | source)
XLA Modules:
  0.0 909.7 jit_solution(15952949547978904606)
XLA Ops:
  7.7 40.2 %collective-permute-done = bf16[3,256,2048]{2,1,0:T(8,128)(2,1)S(1)} collective-permute-done((bf16[3,256,2048]{2,1,0:T(8,128)(2,1)}, bf16[3,256,2048]{2,1,0:T(8,128)(2,1)S(1)}, u32[]{:S(2)}, u32[]{:S(2)}) %collective-permute-start) | collective-permute-done | bytes 3145760 | tf_op jit(solution)/shard_map/ppermute | solution.py:98
  47.9 39.4 %collective-permute-done.1 = bf16[3,256,2048]{2,1,0:T(8,128)(2,1)S(1)} collective-permute-done((bf16[3,256,2048]{2,1,0:T(8,128)(2,1)S(1)}, bf16[3,256,2048]{2,1,0:T(8,128)(2,1)S(1)}, u32[]{:S(2)}, u32[]{:S(2)}) %collective-permute-start.1) | collective-permute-done | bytes 3145760 | tf_op jit(solution)/shard_map/ppermute | solution.py:98
  89.0 39.4 %collective-permute-done.2 = bf16[3,256,2048]{2,1,0:T(8,128)(2,1)S(1)} collective-permute-done((bf16[3,256,2048]{2,1,0:T(8,128)(2,1)S(1)}, bf16[3,256,2048]{2,1,0:T(8,128)(2,1)S(1)}, u32[]{:S(2)}, u32[]{:S(2)}) %collective-permute-start.2) | collective-permute-done | bytes 3145760 | tf_op jit(solution)/shard_map/ppermute | solution.py:98
  130.0 39.4 %collective-permute-done.3 = bf16[3,256,2048]{2,1,0:T(8,128)(2,1)S(1)} collective-permute-done((bf16[3,256,2048]{2,1,0:T(8,128)(2,1)S(1)}, bf16[3,256,2048]{2,1,0:T(8,128)(2,1)S(1)}, u32[]{:S(2)}, u32[]{:S(2)}) %collective-permute-start.3) | collective-permute-done | bytes 3145760 | tf_op jit(solution)/shard_map/ppermute | solution.py:98
  171.0 39.4 %collective-permute-done.4 = bf16[3,256,2048]{2,1,0:T(8,128)(2,1)S(1)} collective-permute-done((bf16[3,256,2048]{2,1,0:T(8,128)(2,1)S(1)}, bf16[3,256,2048]{2,1,0:T(8,128)(2,1)S(1)}, u32[]{:S(2)}, u32[]{:S(2)}) %collective-permute-start.4) | collective-permute-done | bytes 3145760 | tf_op jit(solution)/shard_map/ppermute | solution.py:98
  212.1 39.4 %collective-permute-done.5 = bf16[3,256,2048]{2,1,0:T(8,128)(2,1)S(1)} collective-permute-done((bf16[3,256,2048]{2,1,0:T(8,128)(2,1)S(1)}, bf16[3,256,2048]{2,1,0:T(8,128)(2,1)S(1)}, u32[]{:S(2)}, u32[]{:S(2)}) %collective-permute-start.5) | collective-permute-done | bytes 3145760 | tf_op jit(solution)/shard_map/ppermute | solution.py:98
  253.2 39.4 %collective-permute-done.6 = bf16[3,256,2048]{2,1,0:T(8,128)(2,1)S(1)} collective-permute-done((bf16[3,256,2048]{2,1,0:T(8,128)(2,1)S(1)}, bf16[3,256,2048]{2,1,0:T(8,128)(2,1)S(1)}, u32[]{:S(2)}, u32[]{:S(2)}) %collective-permute-start.6) | collective-permute-done | bytes 3145760 | tf_op jit(solution)/shard_map/ppermute | solution.py:98
  294.3 39.4 %collective-permute-done.7 = bf16[3,256,2048]{2,1,0:T(8,128)(2,1)S(1)} collective-permute-done((bf16[3,256,2048]{2,1,0:T(8,128)(2,1)S(1)}, bf16[3,256,2048]{2,1,0:T(8,128)(2,1)S(1)}, u32[]{:S(2)}, u32[]{:S(2)}) %collective-permute-start.7) | collective-permute-done | bytes 3145760 | tf_op jit(solution)/shard_map/ppermute | solution.py:98
  335.3 39.4 %collective-permute-done.8 = bf16[3,256,2048]{2,1,0:T(8,128)(2,1)S(1)} collective-permute-done((bf16[3,256,2048]{2,1,0:T(8,128)(2,1)S(1)}, bf16[3,256,2048]{2,1,0:T(8,128)(2,1)S(1)}, u32[]{:S(2)}, u32[]{:S(2)}) %collective-permute-start.8) | collective-permute-done | bytes 3145760 | tf_op jit(solution)/shard_map/ppermute | solution.py:98
  376.4 39.4 %collective-permute-done.9 = bf16[3,256,2048]{2,1,0:T(8,128)(2,1)S(1)} collective-permute-done((bf16[3,256,2048]{2,1,0:T(8,128)(2,1)S(1)}, bf16[3,256,2048]{2,1,0:T(8,128)(2,1)S(1)}, u32[]{:S(2)}, u32[]{:S(2)}) %collective-permute-start.9) | collective-permute-done | bytes 3145760 | tf_op jit(solution)/shard_map/ppermute | solution.py:98
  417.4 39.4 %collective-permute-done.10 = bf16[3,256,2048]{2,1,0:T(8,128)(2,1)S(1)} collective-permute-done((bf16[3,256,2048]{2,1,0:T(8,128)(2,1)S(1)}, bf16[3,256,2048]{2,1,0:T(8,128)(2,1)S(1)}, u32[]{:S(2)}, u32[]{:S(2)}) %collective-permute-start.10) | collective-permute-done | bytes 3145760 | tf_op jit(solution)/shard_map/ppermute | solution.py:98
  458.5 39.4 %collective-permute-done.11 = bf16[3,256,2048]{2,1,0:T(8,128)(2,1)S(1)} collective-permute-done((bf16[3,256,2048]{2,1,0:T(8,128)(2,1)S(1)}, bf16[3,256,2048]{2,1,0:T(8,128)(2,1)S(1)}, u32[]{:S(2)}, u32[]{:S(2)}) %collective-permute-start.11) | collective-permute-done | bytes 3145760 | tf_op jit(solution)/shard_map/ppermute | solution.py:98
  499.5 39.5 %collective-permute-done.12 = bf16[3,256,2048]{2,1,0:T(8,128)(2,1)} collective-permute-done((bf16[3,256,2048]{2,1,0:T(8,128)(2,1)S(1)}, bf16[3,256,2048]{2,1,0:T(8,128)(2,1)}, u32[]{:S(2)}, u32[]{:S(2)}) %collective-permute-start.12) | collective-permute-done | bytes 3145760 | tf_op jit(solution)/shard_map/ppermute | solution.py:98
  551.2 2.3 slice.329
  553.5 2.2 broadcast_in_dim.30
  555.7 2.1 reshape.228
  563.3 15.4 %collective-permute-done.13 = bf16[3,256,2048]{2,1,0:T(8,128)(2,1)} collective-permute-done((bf16[3,256,2048]{2,1,0:T(8,128)(2,1)}, bf16[3,256,2048]{2,1,0:T(8,128)(2,1)}, u32[]{:S(2)}, u32[]{:S(2)}) %collective-permute-start.13) | collective-permute-done | bytes 3145760 | tf_op jit(solution)/shard_map/ppermute | solution.py:98
  580.3 4.6 convolution_convert_fusion
  584.9 4.6 convolution_convert_fusion.1
  589.5 12.5 %copy.35 = bf16[128,128,256]{2,1,0:T(8,128)(2,1)} copy(bf16[128,128,256]{0,2,1:T(8,128)(2,1)} %bitcast.135) | data formatting | bytes 16777216 | tf_op jit(solution)/shard_map/while | solution.py:82
  602.0 12.3 %copy.31 = bf16[128,128,256]{2,1,0:T(8,128)(2,1)} copy(bf16[128,128,256]{0,2,1:T(8,128)(2,1)} %bitcast.136) | data formatting | bytes 16777216 | tf_op jit(solution)/shard_map/while | solution.py:82
  618.8 4.0 constant_dynamic-update-slice_fusion.33
  622.8 4.1 constant_dynamic-update-slice_fusion.32
  626.8 4.1 constant_dynamic-update-slice_fusion.31
  637.1 2.1 constant_dynamic-update-slice_fusion.27
  647.5 2.1 constant_dynamic-update-slice_fusion.22
  655.7 2.1 constant_dynamic-update-slice_fusion.18
  657.7 4.0 constant_dynamic-update-slice_fusion.17
  661.7 3.9 constant_dynamic-update-slice_fusion.16
  665.6 4.0 constant_dynamic-update-slice_fusion.15
  669.6 4.0 constant_dynamic-update-slice_fusion.14
  677.6 2.1 constant_dynamic-update-slice_fusion.11
  688.0 2.1 constant_dynamic-update-slice_fusion.6
  698.3 33.5 %fusion.53 = bf16[256,3,2048]{2,0,1:T(8,128)(2,1)S(1)} fusion(bf16[3,8192,2048]{2,1,0:T(8,128)(2,1)} %constant_dynamic-update-slice_fusion.2, s32[]{:T(128)S(6)} %select_n.14, bf16[256,4096]{1,0:T(8,128)(2,1)} %all-gather.2.cloned.1.call-done), kind=kOutput, calls=%fused_computation.77 | convolution fusion | flops 12886474752 | bytes 55574532 | tf_op jit(solution)/shard_map/sd,jdc->sjc/dot_general | solution.py:102
  734.1 5.1 fusion.57
  743.3 4.0 collective-permute-start.17
  752.9 17.0 %while.21 = (s32[]{:T(128)}, f32[2,128,2048]{2,1,0:T(8,128)}, bf16[2,256,2048]{1,2,0:T(8,128)(2,1)}, s32[2,128]{1,0:T(2,128)S(1)}, s32[2,256]{1,0:T(2,128)S(1)}, /*index=5*/bf16[128,128,256]{2,1,0:T(8,128)(2,1)}, s32[]{:T(128)}) while((s32[]{:T(128)}, f32[2,128,2048]{2,1,0:T(8,128)}, bf16[2,256,2048]{1,2,0:T(8,128)(2,1)}, ...), condition=%wide.region_3.4_spmd, body=%wide.region_2.3_spmd.sunk | while | flops 138477568 | bytes 16913496 | solution.py:82
  754.4 5.7 fusion.98
  762.9 5.7 fusion.98
  770.0 21.3 %multiply_add_fusion = f32[384,2,2048]{2,0,1:T(8,128)S(1)} fusion(bf16[256,2,2048]{2,0,1:T(8,128)(2,1)} %slice.413, bf16[136,2,2048]{2,0,1:T(8,128)(2,1)} %collective-permute-done.17, f32[384]{0:T(512)S(1)} %get-tuple-element.172, f32[2,2048]{1,0:T(2,128)S(1)} %get-tuple-element.146, f32[384]{0:T(512)S(1)} %get-tuple-element.173, ...), kind=kLoop, calls=%fused_computation.37 | loop fusion | flops 73924608 | bytes 9626624 | tf_op jit(solution)/shard_map/add | solution.py:25
  798.7 2.8 pad_maximum_fusion.3
  803.1 17.0 %while.20 = (s32[]{:T(128)}, f32[2,128,2048]{2,1,0:T(8,128)}, bf16[2,256,2048]{1,2,0:T(8,128)(2,1)}, s32[2,128]{1,0:T(2,128)S(1)}, s32[2,256]{1,0:T(2,128)S(1)}, /*index=5*/bf16[128,128,256]{2,1,0:T(8,128)(2,1)}, s32[]{:T(128)}) while((s32[]{:T(128)}, f32[2,128,2048]{2,1,0:T(8,128)}, bf16[2,256,2048]{1,2,0:T(8,128)(2,1)}, ...), condition=%wide.region_1.2_spmd, body=%wide.region_0.1_spmd.sunk | while | flops 138477568 | bytes 16913496 | solution.py:82
  804.5 5.7 fusion.94
  813.0 5.7 fusion.94
  820.0 4.2 fusion.56
  826.0 3.6 collective-permute-done.20
  831.6 31.5 %fusion.21 = bf16[256,4096]{1,0:T(8,128)(2,1)} fusion(bf16[3,8192,2048]{2,1,0:T(8,128)(2,1)} %constant_dynamic-update-slice_fusion.2, s32[]{:T(128)S(6)} %select_n.14, bf16[264,3,2048]{2,0,1:T(8,128)(2,1)} %pad_maximum_fusion, f32[256]{0:T(256)S(1)} %copy-done.52, f32[3,2048]{1,0:T(4,128)S(1)} %copy-done.44, f32[256]{0:T(256)S(1)} %copy-done.53, ...), kind=kOutput, calls=%fused_computation.39 | convolution fusion | flops 12931563520 | bytes 74627072 | tf_op jit(solution)/shard_map/sjc,jdc->sd/dot_general | solution.py:146
  863.1 39.5 %reduce-scatter.2.cloned.1.call-done = bf16[256,2048]{1,0:T(8,128)(2,1)} async-done(((bf16[256,4096]{1,0:T(8,128)(2,1)}), bf16[256,2048]{1,0:T(8,128)(2,1)}) %reduce-scatter.2.cloned.1.call-update) | async-done | bytes 1048592 | tf_op jit(solution)/shard_map/reduce_scatter | solution.py:147
  (233 shorter events, 119.0 us)
Async XLA Ops:
  7.2 573.1 %copy-start = (bf16[128,128]{1,0:T(8,128)(2,1)S(1)}, bf16[128,128]{1,0:T(8,128)(2,1)}, u32[]{:S(2)}) copy-start(bf16[128,128]{1,0:T(8,128)(2,1)} %param.13) | copy-start | bytes 98308
  7.2 691.1 %all-gather.2.cloned.1.call-start = ((), (), s32[]{:S(2)}) async-start(), calls=%async_computation.1 | async-start | bytes 3145728 | tf_op jit(solution)/shard_map/all_gather | solution.py:91
  7.2 40.7 %collective-permute-start = (bf16[3,256,2048]{2,1,0:T(8,128)(2,1)}, bf16[3,256,2048]{2,1,0:T(8,128)(2,1)S(1)}, u32[]{:S(2)}, u32[]{:S(2)}) collective-permute-start(bf16[3,256,2048]{2,1,0:T(8,128)(2,1)} %param.11), channel_id=1, source_target_pairs={{0,2},{2,4},{4,6},{6,8},{8,10},{10,12},{12,14},{14,16},{16,18},{18... | collective-permute-start | bytes 9437192 | tf_op jit(solution)/shard_map/ppermute | solution.py:98
  47.9 39.4 %collective-permute-start.1 = (bf16[3,256,2048]{2,1,0:T(8,128)(2,1)S(1)}, bf16[3,256,2048]{2,1,0:T(8,128)(2,1)S(1)}, u32[]{:S(2)}, u32[]{:S(2)}) collective-permute-start(bf16[3,256,2048]{2,1,0:T(8,128)(2,1)S(1)} %collective-permute-done), channel_id=1, source_target_pairs={{0,2},{2,4},{4,6},{6,8},{8,10},{10,12},{12,14},{14,16},{16,18},{18... | collective-permute-start | bytes 9437192 | tf_op jit(solution)/shard_map/ppermute | solution.py:98
  89.0 39.4 %collective-permute-start.2 = (bf16[3,256,2048]{2,1,0:T(8,128)(2,1)S(1)}, bf16[3,256,2048]{2,1,0:T(8,128)(2,1)S(1)}, u32[]{:S(2)}, u32[]{:S(2)}) collective-permute-start(bf16[3,256,2048]{2,1,0:T(8,128)(2,1)S(1)} %collective-permute-done.1), channel_id=1, source_target_pairs={{0,2},{2,4},{4,6},{6,8},{8,10},{10,12},{12,14},{14,16},{16,18},{18... | collective-permute-start | bytes 9437192 | tf_op jit(solution)/shard_map/ppermute | solution.py:98
  130.0 39.4 %collective-permute-start.3 = (bf16[3,256,2048]{2,1,0:T(8,128)(2,1)S(1)}, bf16[3,256,2048]{2,1,0:T(8,128)(2,1)S(1)}, u32[]{:S(2)}, u32[]{:S(2)}) collective-permute-start(bf16[3,256,2048]{2,1,0:T(8,128)(2,1)S(1)} %collective-permute-done.2), channel_id=1, source_target_pairs={{0,2},{2,4},{4,6},{6,8},{8,10},{10,12},{12,14},{14,16},{16,18},{18... | collective-permute-start | bytes 9437192 | tf_op jit(solution)/shard_map/ppermute | solution.py:98
  171.0 39.4 %collective-permute-start.4 = (bf16[3,256,2048]{2,1,0:T(8,128)(2,1)S(1)}, bf16[3,256,2048]{2,1,0:T(8,128)(2,1)S(1)}, u32[]{:S(2)}, u32[]{:S(2)}) collective-permute-start(bf16[3,256,2048]{2,1,0:T(8,128)(2,1)S(1)} %collective-permute-done.3), channel_id=1, source_target_pairs={{0,2},{2,4},{4,6},{6,8},{8,10},{10,12},{12,14},{14,16},{16,18},{18... | collective-permute-start | bytes 9437192 | tf_op jit(solution)/shard_map/ppermute | solution.py:98
  212.1 39.4 %collective-permute-start.5 = (bf16[3,256,2048]{2,1,0:T(8,128)(2,1)S(1)}, bf16[3,256,2048]{2,1,0:T(8,128)(2,1)S(1)}, u32[]{:S(2)}, u32[]{:S(2)}) collective-permute-start(bf16[3,256,2048]{2,1,0:T(8,128)(2,1)S(1)} %collective-permute-done.4), channel_id=1, source_target_pairs={{0,2},{2,4},{4,6},{6,8},{8,10},{10,12},{12,14},{14,16},{16,18},{18... | collective-permute-start | bytes 9437192 | tf_op jit(solution)/shard_map/ppermute | solution.py:98
  253.2 39.4 %collective-permute-start.6 = (bf16[3,256,2048]{2,1,0:T(8,128)(2,1)S(1)}, bf16[3,256,2048]{2,1,0:T(8,128)(2,1)S(1)}, u32[]{:S(2)}, u32[]{:S(2)}) collective-permute-start(bf16[3,256,2048]{2,1,0:T(8,128)(2,1)S(1)} %collective-permute-done.5), channel_id=1, source_target_pairs={{0,2},{2,4},{4,6},{6,8},{8,10},{10,12},{12,14},{14,16},{16,18},{18... | collective-permute-start | bytes 9437192 | tf_op jit(solution)/shard_map/ppermute | solution.py:98
  294.3 39.4 %collective-permute-start.7 = (bf16[3,256,2048]{2,1,0:T(8,128)(2,1)S(1)}, bf16[3,256,2048]{2,1,0:T(8,128)(2,1)S(1)}, u32[]{:S(2)}, u32[]{:S(2)}) collective-permute-start(bf16[3,256,2048]{2,1,0:T(8,128)(2,1)S(1)} %collective-permute-done.6), channel_id=1, source_target_pairs={{0,2},{2,4},{4,6},{6,8},{8,10},{10,12},{12,14},{14,16},{16,18},{18... | collective-permute-start | bytes 9437192 | tf_op jit(solution)/shard_map/ppermute | solution.py:98
  335.3 39.4 %collective-permute-start.8 = (bf16[3,256,2048]{2,1,0:T(8,128)(2,1)S(1)}, bf16[3,256,2048]{2,1,0:T(8,128)(2,1)S(1)}, u32[]{:S(2)}, u32[]{:S(2)}) collective-permute-start(bf16[3,256,2048]{2,1,0:T(8,128)(2,1)S(1)} %collective-permute-done.7), channel_id=1, source_target_pairs={{0,2},{2,4},{4,6},{6,8},{8,10},{10,12},{12,14},{14,16},{16,18},{18... | collective-permute-start | bytes 9437192 | tf_op jit(solution)/shard_map/ppermute | solution.py:98
  376.4 39.4 %collective-permute-start.9 = (bf16[3,256,2048]{2,1,0:T(8,128)(2,1)S(1)}, bf16[3,256,2048]{2,1,0:T(8,128)(2,1)S(1)}, u32[]{:S(2)}, u32[]{:S(2)}) collective-permute-start(bf16[3,256,2048]{2,1,0:T(8,128)(2,1)S(1)} %collective-permute-done.8), channel_id=1, source_target_pairs={{0,2},{2,4},{4,6},{6,8},{8,10},{10,12},{12,14},{14,16},{16,18},{18... | collective-permute-start | bytes 9437192 | tf_op jit(solution)/shard_map/ppermute | solution.py:98
  417.4 39.4 %collective-permute-start.10 = (bf16[3,256,2048]{2,1,0:T(8,128)(2,1)S(1)}, bf16[3,256,2048]{2,1,0:T(8,128)(2,1)S(1)}, u32[]{:S(2)}, u32[]{:S(2)}) collective-permute-start(bf16[3,256,2048]{2,1,0:T(8,128)(2,1)S(1)} %collective-permute-done.9), channel_id=1, source_target_pairs={{0,2},{2,4},{4,6},{6,8},{8,10},{10,12},{12,14},{14,16},{16,18},{18... | collective-permute-start | bytes 9437192 | tf_op jit(solution)/shard_map/ppermute | solution.py:98
  458.5 39.4 %collective-permute-start.11 = (bf16[3,256,2048]{2,1,0:T(8,128)(2,1)S(1)}, bf16[3,256,2048]{2,1,0:T(8,128)(2,1)S(1)}, u32[]{:S(2)}, u32[]{:S(2)}) collective-permute-start(bf16[3,256,2048]{2,1,0:T(8,128)(2,1)S(1)} %collective-permute-done.10), channel_id=1, source_target_pairs={{0,2},{2,4},{4,6},{6,8},{8,10},{10,12},{12,14},{14,16},{16,18},{18... | collective-permute-start | bytes 9437192 | tf_op jit(solution)/shard_map/ppermute | solution.py:98
  499.5 39.5 %collective-permute-start.12 = (bf16[3,256,2048]{2,1,0:T(8,128)(2,1)S(1)}, bf16[3,256,2048]{2,1,0:T(8,128)(2,1)}, u32[]{:S(2)}, u32[]{:S(2)}) collective-permute-start(bf16[3,256,2048]{2,1,0:T(8,128)(2,1)S(1)} %collective-permute-done.11), channel_id=1, source_target_pairs={{0,2},{2,4},{4,6},{6,8},{8,10},{10,12},{12,14},{14,16},{16,18},{18... | collective-permute-start | bytes 9437192 | tf_op jit(solution)/shard_map/ppermute | solution.py:98
  539.0 39.7 %collective-permute-start.13 = (bf16[3,256,2048]{2,1,0:T(8,128)(2,1)}, bf16[3,256,2048]{2,1,0:T(8,128)(2,1)}, u32[]{:S(2)}, u32[]{:S(2)}) collective-permute-start(bf16[3,256,2048]{2,1,0:T(8,128)(2,1)} %collective-permute-done.12), channel_id=1, source_target_pairs={{0,2},{2,4},{4,6},{6,8},{8,10},{10,12},{12,14},{14,16},{16,18},{18... | collective-permute-start | bytes 9437192 | tf_op jit(solution)/shard_map/ppermute | solution.py:98
  539.1 363.5 %reduce-scatter.2.cloned.1.call-start = ((), (), s32[]{:S(2)}) async-start(), calls=%async_computation.2 | async-start | bytes 3145728 | tf_op jit(solution)/shard_map/reduce_scatter | solution.py:147
  540.4 74.5 %collective-permute-start.16 = (s32[136]{0:T(256)}, s32[136]{0:T(256)}, u32[]{:S(2)}, u32[]{:S(2)}) collective-permute-start(s32[136]{0:T(256)} %slice.310), channel_id=1, source_target_pairs={{0,2},{2,4},{4,6},{6,8},{8,10},{10,12},{12,14},{14,16},{16,18},{18... | collective-permute-start | bytes 1640 | tf_op jit(solution)/shard_map/ppermute | solution.py:10
  543.5 70.7 %collective-permute-start.19 = (s32[128]{0:T(128)}, s32[128]{0:T(128)}, u32[]{:S(2)}, u32[]{:S(2)}) collective-permute-start(s32[128]{0:T(128)} %slice.367), channel_id=1, source_target_pairs={{2,0},{4,2},{6,4},{8,6},{10,8},{12,10},{14,12},{16,14},{18,16},{20... | collective-permute-start | bytes 1544 | tf_op jit(solution)/shard_map/ppermute | solution.py:10
  578.7 40.1 %collective-permute-start.14 = (bf16[3,256,2048]{2,1,0:T(8,128)(2,1)}, bf16[3,256,2048]{2,1,0:T(8,128)(2,1)}, u32[]{:S(2)}, u32[]{:S(2)}) collective-permute-start(bf16[3,256,2048]{2,1,0:T(8,128)(2,1)} %collective-permute-done.13), channel_id=1, source_target_pairs={{0,2},{2,4},{4,6},{6,8},{8,10},{10,12},{12,14},{14,16},{16,18},{18... | collective-permute-start | bytes 9437192 | tf_op jit(solution)/shard_map/ppermute | solution.py:98
  602.0 12.3 %copy-start.36 = (s32[256]{0:T(256)S(1)}, s32[256]{0:T(256)}, u32[]{:S(2)}) copy-start(s32[256]{0:T(256)} %param.14) | copy-start | bytes 3076
  622.8 8.2 copy-start.24
  698.2 35.8 %copy-start.37 = (f32[2048,1]{0,1:T(1,128)S(1)}, f32[2048,1]{0,1:T(1,128)}, u32[]{:S(2)}) copy-start(f32[2048,1]{0,1:T(1,128)} %get-tuple-element.152) | copy-start | bytes 24580
  698.2 35.8 %copy-start.38 = (f32[2048,1]{0,1:T(1,128)S(1)}, f32[2048,1]{0,1:T(1,128)}, u32[]{:S(2)}) copy-start(f32[2048,1]{0,1:T(1,128)} %get-tuple-element.153) | copy-start | bytes 24580
  698.3 35.8 %copy-start.39 = (f32[2048,1]{0,1:T(1,128)S(1)}, f32[2048,1]{0,1:T(1,128)}, u32[]{:S(2)}) copy-start(f32[2048,1]{0,1:T(1,128)} %get-tuple-element.154) | copy-start | bytes 24580
  698.3 35.8 %copy-start.40 = (f32[2048,1]{0,1:T(1,128)S(1)}, f32[2048,1]{0,1:T(1,128)}, u32[]{:S(2)}) copy-start(f32[2048,1]{0,1:T(1,128)} %get-tuple-element.155) | copy-start | bytes 24580
  698.3 35.8 %copy-start.41 = (f32[2048,1]{0,1:T(1,128)S(1)}, f32[2048,1]{0,1:T(1,128)}, u32[]{:S(2)}) copy-start(f32[2048,1]{0,1:T(1,128)} %get-tuple-element.156) | copy-start | bytes 24580
  698.3 35.8 %copy-start.42 = (f32[2048,1]{0,1:T(1,128)S(1)}, f32[2048,1]{0,1:T(1,128)}, u32[]{:S(2)}) copy-start(f32[2048,1]{0,1:T(1,128)} %get-tuple-element.157) | copy-start | bytes 24580
  698.3 35.8 %copy-start.43 = (f32[2048,1]{0,1:T(1,128)S(1)}, f32[2048,1]{0,1:T(1,128)}, u32[]{:S(2)}) copy-start(f32[2048,1]{0,1:T(1,128)} %get-tuple-element.158) | copy-start | bytes 24580
  731.9 2.1 collective-permute-start.15
  739.3 8.6 collective-permute-start.18
  743.3 26.7 %collective-permute-start.17 = (bf16[136,2,2048]{2,0,1:T(8,128)(2,1)}, bf16[136,2,2048]{2,0,1:T(8,128)(2,1)}, u32[]{:S(2)}, u32[]{:S(2)}) collective-permute-start(bf16[136,2,2048]{2,0,1:T(8,128)(2,1)} %slice.412), channel_id=1, source_target_pairs={{0,2},{2,4},{4,6},{6,8},{8,10},{10,12},{12,14},{14,16},{16,18},{18... | collective-permute-start | bytes 3342344 | tf_op jit(solution)/shard_map/ppermute | solution.py:10
  752.9 17.0 %copy-start.32 = (f32[2,2048]{1,0:T(2,128)S(1)}, f32[2,2048]{1,0:T(2,128)}, u32[]{:S(2)}) copy-start(f32[2,2048]{1,0:T(2,128)} %get-tuple-element.148) | copy-start | bytes 49156
  752.9 17.0 %copy-start.33 = (f32[2,2048]{1,0:T(2,128)S(1)}, f32[2,2048]{1,0:T(2,128)}, u32[]{:S(2)}) copy-start(f32[2,2048]{1,0:T(2,128)} %get-tuple-element.149) | copy-start | bytes 49156
  752.9 17.0 %copy-start.34 = (f32[2,2048]{1,0:T(2,128)S(1)}, f32[2,2048]{1,0:T(2,128)}, u32[]{:S(2)}) copy-start(f32[2,2048]{1,0:T(2,128)} %get-tuple-element.150) | copy-start | bytes 49156
  752.9 17.1 %copy-start.35 = (f32[2,2048]{1,0:T(2,128)S(1)}, f32[2,2048]{1,0:T(2,128)}, u32[]{:S(2)}) copy-start(f32[2,2048]{1,0:T(2,128)} %get-tuple-element.151) | copy-start | bytes 49156
  824.2 7.3 copy-start.44
  824.2 7.3 copy-start.45
  824.2 7.3 copy-start.46
  824.2 7.3 copy-start.47
  824.2 7.3 copy-start.48
  824.2 7.3 copy-start.49
  824.2 7.3 copy-start.50
  824.3 7.3 copy-start.51
  824.3 7.3 copy-start.52
  824.3 7.3 copy-start.53
  824.6 5.0 collective-permute-start.20
  831.6 71.0 %copy-start.1 = (bf16[128,128]{1,0:T(8,128)(2,1)S(1)}, bf16[128,128]{1,0:T(8,128)(2,1)}, u32[]{:S(2)}) copy-start(bf16[128,128]{1,0:T(8,128)(2,1)} %param.13) | copy-start | bytes 98308
  (29 other events, 98.3 us)
Sparse Core Ops, SparseCore 0:
  539.2 34.7 all-gather.1
  863.2 39.3 reduce-scatter.1
